TPU v7x, 32 devices: a whole 2x2x4 slice. The times are simulated.
32 devices in a mesh: mp: 2 (over x), row: 16 (over z, y, core).
Axes of the slice: x: 2, y: 2, z: 4, core: 2. Of those that a mesh axis runs over, the one named last changes fastest.
Arguments:
- radial_funcs: bfloat16 [128, 1024], P('row'), may hold values from -6 to 6
- kernels: bfloat16 [80, 1024], P('mp'), parts along dimension 0, may hold values from -0.0010299683 to 0.0010299683
- wigner: float32 [40, 128], replicated, may hold values from -4 to 4
- sources: bfloat16 [64, 2048], P('mp', 'row'), parts along dimension 0, may hold values from -6 to 6
- wigner_slots: int32 [2048], P('row'), may hold values from 0 to 127
- owners: int32 [2048], P('row'), may hold values from 0 to 7, as said below
- degrees: int32 [128], P('row'), may hold values from 0 to 30
- frequencies: float32 [2048], P('row'), may hold values from 0.5 to 2
Outputs:
- response: float32 [64, 2048], P('mp', 'row'), parts along dimension 0
There are 2 independent parts, one for each index of `mp`. A program takes and returns all parts, laid end to end along the dimension named above; an argument that names none is the same for every part. Nothing has to cross between parts.
Inputs may be any that keep to these rules, and one draw needn't show every extreme that they name: Within each aligned block of 128 singlets, owners never falls and every value 0 to 7 occurs.
All inputs are finite; a program needn't handle non-finite values.
Results may differ from a plain program's by a relative error of at most 0.0055.
Values may be sent and summed in bfloat16 or wider, within the bound.
A program may use at most 128 MiB of HBM per device.

v0:
```python
import jax
import jax.numpy as jnp
from jax import lax
from jax.sharding import PartitionSpec as P


def lookup(wigner, slot_block):
    return jnp.take(wigner, slot_block, axis=1)


def project(source_block, slot_block, owner_block, wigner, mult_dev):
    angular = lookup(wigner, slot_block)
    member = (owner_block[:, None] == jnp.arange(mult_dev, dtype=jnp.int32)[None, :]).astype(
        jnp.float32
    )
    scaled = angular[:, None, :] * source_block.astype(jnp.float32)[None, :, :]
    return jnp.einsum("skj,ja->ska", scaled, member, precision=lax.Precision.HIGHEST)


def selection(near_deg, far_deg, num_degree):
    level = jnp.arange(num_degree, dtype=jnp.int32)[:, None, None]
    total_deg = near_deg[None, :, None] + far_deg[None, None, :]
    diff_deg = jnp.abs(near_deg[None, :, None] - far_deg[None, None, :])
    return (diff_deg <= level) & (level <= total_deg) & ((total_deg + level) % 2 == 0)


def local(radial_funcs, kernels, wigner, sources, wigner_slots, owners, degrees, frequencies):
    num_degree = kernels.shape[0]
    mult_dev = radial_funcs.shape[0]
    own_part = project(sources, wigner_slots, owners, wigner, mult_dev).astype(jnp.bfloat16)
    projected, deg_all = (
        lax.all_gather(own_part, "row", axis=2, tiled=True),
        lax.all_gather(degrees, "row", axis=0, tiled=True),
    )
    weighted = (
        radial_funcs.astype(jnp.float32)[None] * kernels.astype(jnp.float32)[:, None, :]
    ).astype(jnp.bfloat16)
    weighted = weighted.reshape(num_degree * mult_dev, radial_funcs.shape[1])
    fetched = lax.all_gather(radial_funcs, "row", axis=0, tiled=True)
    piece_rows = fetched.shape[0]
    integral = lax.dot_general(
        weighted, fetched, (((1,), (1,)), ((), ())), preferred_element_type=jnp.float32
    )
    integral = integral.reshape(num_degree, mult_dev, piece_rows)
    kept_block = jnp.where(
        selection(degrees, deg_all, num_degree), integral, jnp.float32(0.0)
    ).astype(jnp.bfloat16)
    coupled = jnp.einsum("sab,skb->ska", kept_block, projected, preferred_element_type=jnp.float32)
    angular = lookup(wigner, wigner_slots)
    member = (owners[None, :] == jnp.arange(mult_dev, dtype=jnp.int32)[:, None]).astype(jnp.float32)
    spread = jnp.einsum("ska,ai->ski", coupled, member, precision=lax.Precision.HIGHEST)
    return frequencies[None, :] * sources.astype(jnp.float32) + jnp.sum(
        angular[:, None, :] * spread, axis=0
    )


def solution(mesh):
    in_specs = (
        P("row", None),
        P("mp", None),
        P(),
        P("mp", "row"),
        P("row"),
        P("row"),
        P("row"),
        P("row"),
    )
    out_specs = P("mp", "row")
    return jax.shard_map(local, mesh=mesh, in_specs=in_specs, out_specs=out_specs, check_vma=False)
```

profile of v0, /device:TPU:1, one launch (start us, length us, event | category | flops | bytes accessed | tf_op | source)
XLA Modules:
  0.0 67.6 jit_solution(15264262395300003951)
XLA Ops:
  0.0 0.8 %copy.11 = f32[40,128]{0,1:T(8,128)S(1)} copy(f32[40,128]{1,0:T(8,128)} %param.12) | data formatting | bytes 40960 | tf_op args[2]
  0.8 0.7 compare_select_fusion
  1.5 0.6 gather_fusion
  2.1 0.7 compare_and_fusion
  2.8 0.1 select_bitcast_fusion
  2.9 0.1 copy.12
  2.9 0.7 %convert_element_type.23 = f32[32,128]{1,0:T(8,128)S(1)} convert(bf16[32,128]{1,0:T(8,128)(2,1)} %param.13) | non-fusion elementwise | flops 4096 | bytes 24576 | tf_op jit(solution)/shard_map/convert_element_type | solution.py:52
  3.7 2.1 %fusion.7 = bf16[40,32,8]{1,2,0:T(8,128)(2,1)S(1)} fusion(f32[32,128]{1,0:T(8,128)S(1)} %convert_element_type.23, f32[40,128]{1,0:T(8,128)S(1)} %copy.12, s32[128]{0:T(128)} %param.15), kind=kOutput, calls=%fused_computation.9 | convolution fusion | flops 15893504 | bytes 57856 | tf_op jit(solution)/shard_map/skj,ja->ska/dot_general | solution.py:17
  5.8 0.1 copy.13
  5.9 0.0 copy-start.6
  5.9 0.0 copy-start.3
  6.0 0.0 copy-start.1
  6.0 26.1 %all_gather.9 = bf16[40,32,128]{0,1,2:T(8,128)(2,1)S(1)} all-gather(bf16[40,32,8]{0,1,2:T(8,128)(2,1)S(1)} %copy.13), channel_id=1, replica_groups=mesh['mp'=2,'row'=16] {'row'}, dimensions={2}, use_global_device_ids=true | all-gather | bytes 348160 | tf_op jit(solution)/shard_map/all_gather | solution.py:32
  32.1 0.0 copy-start
  32.1 1.4 %copy.14 = bf16[40,32,128]{2,1,0:T(8,128)(2,1)S(1)} copy(bf16[40,32,128]{0,1,2:T(8,128)(2,1)S(1)} %all_gather.9) | data formatting | bytes 655360 | tf_op jit(solution)/shard_map/all_gather | solution.py:32
  33.5 0.0 copy-done.6
  33.5 0.6 dynamic-slice
  34.7 0.0 copy-done.3
  34.7 0.2 dynamic-update-slice
  35.0 4.1 %all-reduce = s32[128]{0:T(128)S(1)} all-reduce(s32[128]{0:T(128)S(1)} %dynamic-update-slice), channel_id=1, replica_groups=mesh['mp'=2,'row'=16] {'row'}, use_global_device_ids=true, to_apply=%add | all-reduce | flops 128 | bytes 1024
  39.1 0.1 subtract_abs_fusion
  39.1 0.0 copy-done.1
  39.1 26.2 %all_gather.11 = bf16[128,1024]{1,0:T(8,128)(2,1)S(1)} all-gather(bf16[8,1024]{1,0:T(8,128)(2,1)S(1)} %copy-done.1), channel_id=1, replica_groups=mesh['mp'=2,'row'=16] {'row'}, dimensions={0}, use_global_device_ids=true | all-gather | bytes 278528 | tf_op jit(solution)/shard_map/all_gather | solution.py:39
  65.3 0.0 copy-done
  65.4 0.0 copy-start.2
  65.4 0.0 copy-start.4
  65.4 0.8 %fusion.2 = f32[40,32,8]{1,2,0:T(8,128)S(1)} fusion(bf16[40,32,128]{2,1,0:T(8,128)(2,1)S(1)} %copy.14, f32[40,1024]{1,0:T(8,128)S(1)} %convert_element_type.26, f32[8,1024]{1,0:T(8,128)S(1)} %convert_element_type.25, bf16[128,1024]{1,0:T(8,128)(2,1)S(1)} %all_gather.11, s32[8,128]{1,0:T(8,128)S(1)} %get-tuple-element.7, s32[8,128]{1,0:T(8,128)S(1)} %get-tuple-element.6), kind=kOutput, calls=%fused_computation.6 | convolution fusion | flops 87941120 | bytes 835584 | tf_op jit(solution)/shard_map/sab,skb->ska/dot_general | solution.py:48
  66.2 0.0 copy-done.5
  66.2 0.7 %fusion = f32[32,128]{1,0:T(8,128)S(1)} fusion(f32[40,32,8]{1,2,0:T(8,128)S(1)} %fusion.2, f32[40,128]{1,0:T(8,128)S(1)} %copy.12, s32[128]{0:T(128)S(1)} %copy-done.5), kind=kOutput, calls=%fused_computation.3 | convolution fusion | flops 16053248 | bytes 78336 | tf_op jit(solution)/shard_map/ska,ai->ski/dot_general | solution.py:51
  67.0 0.0 copy-done.2
  67.0 0.0 copy-done.4
  67.0 0.6 multiply_add_fusion
  (5 shorter events, 0.0 us)
Async XLA Ops:
  5.9 27.6 %copy-start.6 = (u32[32]{0:T(128)S(1)}, u32[32]{0:T(128)}, u32[]{:S(2)}) copy-start(u32[32]{0:T(128)} %constant.32) | copy-start | bytes 388
  5.9 28.8 %copy-start.3 = (s32[8]{0:T(128)S(1)}, s32[8]{0:T(128)}, u32[]{:S(2)}) copy-start(s32[8]{0:T(128)} %param.16) | copy-start | bytes 100
  6.0 33.2 %copy-start.1 = (bf16[8,1024]{1,0:T(8,128)(2,1)S(1)}, bf16[8,1024]{1,0:T(8,128)(2,1)}, u32[]{:S(2)}) copy-start(bf16[8,1024]{1,0:T(8,128)(2,1)} %param.10) | copy-start | bytes 49156
  32.1 33.2 %copy-start = (bf16[40,1024]{1,0:T(8,128)(2,1)S(1)}, bf16[40,1024]{1,0:T(8,128)(2,1)}, u32[]{:S(2)}) copy-start(bf16[40,1024]{1,0:T(8,128)(2,1)} %param.11) | copy-start | bytes 245764
  65.3 0.9 %copy-start.5 = (s32[128]{0:T(128)S(1)}, s32[128]{0:T(128)}, u32[]{:S(2)}) copy-start(s32[128]{0:T(128)} %param.15) | copy-start | bytes 1540
  65.4 1.6 %copy-start.2 = (bf16[32,128]{1,0:T(8,128)(2,1)S(1)}, bf16[32,128]{1,0:T(8,128)(2,1)}, u32[]{:S(2)}) copy-start(bf16[32,128]{1,0:T(8,128)(2,1)} %param.13) | copy-start | bytes 24580
  65.4 1.6 %copy-start.4 = (f32[128]{0:T(128)S(1)}, f32[128]{0:T(128)}, u32[]{:S(2)}) copy-start(f32[128]{0:T(128)} %param.17) | copy-start | bytes 1540
where the time goes:
time: 68 us; the launch traced here: 67.6 us
  blocking collectives  56.4 us (83%)
  local copies, waits for them, and re-layouts  3.89 us (6%)
  matrix products  3.68 us (5%)
  other arithmetic  2.84 us (4%)
  between operations  0.79 us (1%)
    all_gather x1, blocking collectives, local(): fetched = lax.all_gather(radial_funcs, 'row', axis=0, tiled=True)  26.2 us
    all_gather x1, blocking collectives, local(): lax.all_gather(own_part, 'row', axis=2, tiled=True)  26.1 us
    unnamed x1, blocking collectives  4.07 us
    dot_general x1, matrix products, project(): jnp.einsum('skj,ja->ska', scaled, member, precision=lax.Precision.HIGHEST)  2.11 us
    unnamed x17, local copies, waits for them, and re-layouts  1.69 us

commit v1 on v0

v1 whole, which is shorter than its diff:
```python
import functools

import jax
import jax.numpy as jnp
from jax import lax
from jax.experimental import pallas as pl
from jax.experimental.pallas import tpu as pltpu
from jax.sharding import PartitionSpec as P

MESH = pl.DeviceIdType.MESH
BF16 = jnp.bfloat16
F32 = jnp.float32
I32 = jnp.int32
LANES = 128


def grid_of(n):
    chips = n // 2
    inner = max(d for d in range(1, chips + 1) if chips % d == 0 and d * d <= chips)
    return chips // inner, inner


def halves(value):
    high = value.astype(BF16)
    return high, (value - high.astype(F32)).astype(BF16)


def kernel(
    n, rad_ref, ker_ref, wig_ref, src_ref, slot_ref, own_ref, deg_ref, freq_ref,
    out_ref, fbuf, pbuf, send_sem, recv_sem,
):
    outer, inner = grid_of(n)
    me = lax.axis_index("row")
    core = lax.rem(me, 2)
    chip = lax.div(me, 2)
    my_in = lax.rem(chip, inner)
    my_out = lax.div(chip, inner)

    def index(o, i, c):
        return (o * inner + i) * 2 + c

    def at_out(step):
        return lax.rem(my_out + step, outer)

    def at_in(step):
        return lax.rem(my_in + step, inner)

    out_peers = [index(at_out(t), my_in, core) for t in range(1, outer)]
    in_peers = [index(my_out, at_in(t), core) for t in range(1, inner)]
    sibling = index(my_out, my_in, 1 - core)
    peers = out_peers + in_peers + [sibling]

    barrier = pltpu.get_barrier_semaphore()
    for peer in peers:
        pl.semaphore_signal(barrier, inc=1, device_id={"row": peer}, device_id_type=MESH)

    bufs = (fbuf, pbuf)
    started = []
    counts = [0, 0]

    def send(part, slot, peer):
        copy = pltpu.make_async_remote_copy(
            src_ref=bufs[part].at[slot],
            dst_ref=bufs[part].at[slot],
            send_sem=send_sem.at[part, counts[part]],
            recv_sem=recv_sem.at[part, slot],
            device_id={"row": peer},
            device_id_type=MESH,
        )
        counts[part] += 1
        copy.start()
        started.append(copy)

    def arrived(part, slot):
        pltpu.make_async_remote_copy(
            src_ref=bufs[part].at[slot],
            dst_ref=bufs[part].at[slot],
            send_sem=send_sem.at[part, 0],
            recv_sem=recv_sem.at[part, slot],
            device_id={"row": sibling},
            device_id_type=MESH,
        ).wait_recv()

    def send_own(part):
        for peer in out_peers + in_peers + [sibling]:
            send(part, me, peer)

    def pass_out(part):
        for slot in out_peers:
            arrived(part, slot)
            for peer in in_peers + [sibling]:
                send(part, slot, peer)

    def pass_in(part):
        for o in range(outer):
            for i in range(1, inner):
                slot = index(at_out(o), at_in(i), core)
                arrived(part, slot)
                send(part, slot, sibling)

    def last(part):
        for o in range(outer):
            for i in range(inner):
                arrived(part, index(at_out(o), at_in(i), 1 - core))

    mult, nodes = rad_ref.shape
    num_degree, table = wig_ref.shape
    nsrc, width = src_ref.shape
    half_nodes = nodes // 2
    half_deg = num_degree // 2
    half_lanes = half_deg * nsrc

    rad = rad_ref[...].astype(F32)
    deg_row = deg_ref[...].astype(F32)
    eye = lax.broadcasted_iota(I32, (mult, mult), 0) == lax.broadcasted_iota(I32, (mult, mult), 1)
    deg_col = jnp.sum(jnp.where(eye, deg_row, 0.0), axis=1, keepdims=True)
    deg_block = jnp.broadcast_to(deg_col, (mult, LANES))
    fbuf[me, :, :half_nodes] = jnp.concatenate(
        [rad[:, :half_nodes], rad[:, half_nodes:]], axis=0
    ).astype(BF16)
    fbuf[me, :, half_nodes:] = jnp.concatenate([deg_block, deg_block], axis=0).astype(BF16)
    pl.semaphore_wait(barrier, len(peers))
    send_own(0)

    hot = (lax.broadcasted_iota(I32, (table, width), 0) == slot_ref[...]).astype(F32).astype(BF16)
    wig_high, wig_low = halves(wig_ref[...])
    angular = jnp.dot(wig_high, hot, preferred_element_type=F32) + jnp.dot(
        wig_low, hot, preferred_element_type=F32
    )
    member = (lax.broadcasted_iota(I32, (mult, width), 0) == own_ref[...]).astype(F32)
    src = src_ref[...].astype(F32)
    scaled = (angular[:, None, :] * src[None, :, :]).reshape(num_degree * nsrc, width)
    scaled_high, scaled_low = halves(scaled)
    member16 = member.astype(BF16)
    dims = (((1,), (1,)), ((), ()))
    own_part = lax.dot_general(
        jnp.concatenate([member16, member16], axis=1),
        jnp.concatenate([scaled_high, scaled_low], axis=1),
        dims,
        preferred_element_type=F32,
    )
    pbuf[me] = jnp.concatenate(
        [own_part[:, :half_lanes], own_part[:, half_lanes:]], axis=0
    ).astype(BF16)
    send_own(1)

    pass_out(0)

    ker = ker_ref[...].astype(F32)
    weighted = (ker[:, None, :] * rad[None, :, :]).reshape(num_degree * mult, nodes).astype(BF16)
    placed = (angular[:, None, :] * member[None, :, :]).reshape(num_degree * mult, width)
    placed_high, placed_low = halves(placed)

    pass_in(0)
    pass_out(1)
    last(0)

    far = n * 2 * mult
    funcs = fbuf[...].reshape(far, half_nodes + LANES)
    ones = jnp.full((mult, LANES), 1.0 / LANES, BF16)
    far_deg = lax.dot_general(
        ones, funcs[:, half_nodes:], dims, preferred_element_type=F32
    ).astype(I32)
    near_deg = deg_col.astype(I32)
    total = near_deg + far_deg
    apart = jnp.abs(near_deg - far_deg)
    odd = total & 1
    second = (lax.broadcasted_iota(I32, (mult, far), 1) & mult) // mult
    never = jnp.int32(1 << 20)
    least = [
        [jnp.where((odd == p) & (second == h), apart, never) for p in range(2)] for h in range(2)
    ]
    top = lax.dot_general(
        weighted[:, :half_nodes], funcs[:, :half_nodes], dims, preferred_element_type=F32
    )
    low = lax.dot_general(
        weighted[:, half_nodes:], funcs[:, :half_nodes], dims, preferred_element_type=F32
    )
    edge = half_deg * mult
    first_sum = top[:edge] + pltpu.roll(low[:edge], far - mult, axis=1)
    second_sum = low[edge:] + pltpu.roll(top[edge:], mult, axis=1)
    rows = []
    for s in range(num_degree):
        h = s // half_deg
        value = (first_sum, second_sum)[h][(s - h * half_deg) * mult:(s - h * half_deg + 1) * mult]
        keep = (least[h][s % 2] <= s) & (total >= s)
        rows.append(jnp.where(keep, value, 0.0))

    pass_in(1)
    last(1)

    per = LANES // nsrc
    lane_of = lax.broadcasted_iota(I32, (per * mult, LANES), 1) // nsrc
    row_of = lax.broadcasted_iota(I32, (per * mult, LANES), 0) // mult
    diagonal = lane_of == row_of
    pieces = [[], []]
    for g in range(half_lanes // LANES):
        lhs = jnp.concatenate(
            [rows[h * half_deg + g * per + t] for h in range(2) for t in range(per)], axis=0
        ).astype(BF16)
        rhs = pbuf[:, :, g * LANES:(g + 1) * LANES].reshape(far, LANES)
        both = jnp.dot(lhs, rhs, preferred_element_type=F32)
        for h in range(2):
            pieces[h].append(jnp.where(diagonal, both[h * per * mult:(h + 1) * per * mult], 0.0))
    coupled = jnp.concatenate(pieces[0] + pieces[1], axis=0)
    coupled_high, coupled_low = halves(coupled)
    spread = lax.dot_general(
        jnp.concatenate([coupled_high, coupled_low, coupled_high], axis=0),
        jnp.concatenate([placed_high, placed_high, placed_low], axis=0),
        (((0,), (0,)), ((), ())),
        preferred_element_type=F32,
    )
    result = freq_ref[...] * src
    for t in range(per):
        result = result + spread[t * nsrc:(t + 1) * nsrc]
    out_ref[...] = result
    for copy in started:
        copy.wait_send()


def local(n, radial_funcs, kernels, wigner, sources, wigner_slots, owners, degrees, frequencies):
    mult, nodes = radial_funcs.shape
    num_degree = kernels.shape[0]
    nsrc, width = sources.shape
    return pl.pallas_call(
        functools.partial(kernel, n),
        out_shape=jax.ShapeDtypeStruct((nsrc, width), F32),
        in_specs=[pl.BlockSpec(memory_space=pltpu.VMEM)] * 8,
        out_specs=pl.BlockSpec(memory_space=pltpu.VMEM),
        scratch_shapes=[
            pltpu.VMEM((n, 2 * mult, nodes // 2 + LANES), BF16),
            pltpu.VMEM((n, 2 * mult, num_degree * nsrc // 2), BF16),
            pltpu.SemaphoreType.DMA((2, n - 1)),
            pltpu.SemaphoreType.DMA((2, n)),
        ],
        compiler_params=pltpu.CompilerParams(
            collective_id=0, has_side_effects=True, vmem_limit_bytes=(8 << 20) + n * (256 << 10)
        ),
    )(
        radial_funcs, kernels, wigner, sources, wigner_slots.reshape(1, -1), owners.reshape(1, -1),
        degrees.reshape(1, -1), frequencies.reshape(1, -1),
    )


def solution(mesh):
    in_specs = (
        P("row", None),
        P("mp", None),
        P(),
        P("mp", "row"),
        P("row"),
        P("row"),
        P("row"),
        P("row"),
    )
    out_specs = P("mp", "row")
    return jax.shard_map(
        functools.partial(local, mesh.shape["row"]),
        mesh=mesh,
        in_specs=in_specs,
        out_specs=out_specs,
        check_vma=False,
    )
```

time: 68 us -> 21.1 us (0.31)
  blocking collectives: 56.4 us -> 0 us
  Pallas kernels: 0 us -> 16.4 us
  matrix products: 3.68 us -> 0 us
  other arithmetic: 2.84 us -> 0 us
  between operations: 0.79 us -> 0.03 us
    all_gather x2 -> x0, blocking collectives: 52.4 us -> none  [the longest x1 26.2 us: local(): fetched = lax.all_gather(radial_funcs, 'row', axis=0, tiled=True)]
    pallas_call x0 -> x1, Pallas kernels: none -> 16.4 us  [local(): pl.pallas_call(functools.partial(kernel, n), out_shape=jax.ShapeDtypeStru...]
    unnamed x1 -> x0, blocking collectives: 4.07 us -> none
    dot_general x3 -> x0, matrix products: 3.68 us -> none  [the longest x1 2.11 us: project(): jnp.einsum('skj,ja->ska', scaled, member, precision=lax.Precision.HIGHEST)]
    unnamed x17, local copies, waits for them, and re-layouts: 1.69 us -> 4.32 us
    all_gather x1 -> x0, local copies, waits for them, and re-layouts: 1.36 us -> none  [local(): lax.all_gather(own_part, 'row', axis=2, tiled=True)]
    select_n x2 -> x0, other arithmetic: 0.75 us -> none  [lookup(): return jnp.take(wigner, slot_block, axis=1)]
    convert_element_type x3 -> x0, other arithmetic: 0.74 us -> none  [the longest x1 0.72 us: local(): sources.astype(jnp.float32)]
where the time goes in v1:
time: 21.1 us; the launch traced here: 20.8 us
  Pallas kernels  16.4 us (78%)
  local copies, waits for them, and re-layouts  4.32 us (20%)
    pallas_call x1, Pallas kernels, local(): pl.pallas_call(functools.partial(kernel, n), out_shape=jax.ShapeDtypeStru...  16.4 us
    unnamed x17, local copies, waits for them, and re-layouts  4.32 us

profile of v1, /device:TPU:1, one launch (start us, length us, event | category | flops | bytes accessed | tf_op | source)
XLA Modules:
  0.0 20.8 jit_solution(3630329139904480229)
XLA Ops:
  0.0 0.0 copy-start.7
  0.0 0.0 copy-start.4
  0.0 0.0 copy-start.5
  0.0 0.0 copy-start.6
  0.0 0.6 %copy-done.7 = f32[128]{0:T(128)S(1)} copy-done((f32[128]{0:T(128)S(1)}, f32[128]{0:T(128)}, u32[]{:S(2)}) %copy-start.7) | copy-done | bytes 536
  0.7 0.0 copy-done.4
  0.7 0.0 copy-done.5
  0.7 0.0 copy-done.6
  0.7 0.0 copy-start
  0.7 0.9 %copy-done = bf16[40,1024]{1,0:T(8,128)(2,1)S(1)} copy-done((bf16[40,1024]{1,0:T(8,128)(2,1)S(1)}, bf16[40,1024]{1,0:T(8,128)(2,1)}, u32[]{:S(2)}) %copy-start) | copy-done | bytes 81944
  1.6 0.0 copy-start.1
  1.6 0.7 %copy-done.1 = f32[40,128]{1,0:T(8,128)S(1)} copy-done((f32[40,128]{1,0:T(8,128)S(1)}, f32[40,128]{1,0:T(8,128)}, u32[]{:S(2)}) %copy-start.1) | copy-done | bytes 20504
  2.3 0.0 copy-start.2
  2.3 0.7 %copy-done.2 = bf16[8,1024]{1,0:T(8,128)(2,1)S(1)} copy-done((bf16[8,1024]{1,0:T(8,128)(2,1)S(1)}, bf16[8,1024]{1,0:T(8,128)(2,1)}, u32[]{:S(2)}) %copy-start.2) | copy-done | bytes 16408
  3.0 0.0 copy-start.3
  3.0 0.7 %copy-done.3 = bf16[32,128]{1,0:T(8,128)(2,1)S(1)} copy-done((bf16[32,128]{1,0:T(8,128)(2,1)S(1)}, bf16[32,128]{1,0:T(8,128)(2,1)}, u32[]{:S(2)}) %copy-start.3) | copy-done | bytes 8216
  3.7 16.4 %shard_map.82 = f32[32,128]{1,0:T(8,128)S(1)} custom-call(bf16[8,1024]{1,0:T(8,128)(2,1)S(1)} %copy-done.2, bf16[40,1024]{1,0:T(8,128)(2,1)S(1)} %copy-done, f32[40,128]{1,0:T(8,128)S(1)} %copy-done.1, bf16[32,128]{1,0:T(8,128)(2,1)S(1)} %copy-done.3, s32[1,128]{1,0:T(1,128)S(1)} %bitcast.4, s32[1,128]{1,0:T(1,128)S(1)} %bitcast.5, s32[1,8]{1,0:T(1,128)S(1)} %bitcast.6, ...), custom_call_target="tpu_custom_call" | custom-call | tf_op jit(solution)/shard_map/pallas_call | solution.py:225
  20.2 0.6 %copy.10 = f32[32,128]{1,0:T(8,128)} copy(f32[32,128]{1,0:T(8,128)S(1)} %shard_map.82) | data formatting | bytes 32768
Async XLA Ops:
  0.0 0.7 %copy-start.7 = (f32[128]{0:T(128)S(1)}, f32[128]{0:T(128)}, u32[]{:S(2)}) copy-start(f32[128]{0:T(128)} %param.15) | copy-start | bytes 1540
  0.0 0.7 %copy-start.4 = (s32[128]{0:T(128)S(1)}, s32[128]{0:T(128)}, u32[]{:S(2)}) copy-start(s32[128]{0:T(128)} %param.12) | copy-start | bytes 1540
  0.0 0.7 %copy-start.5 = (s32[128]{0:T(128)S(1)}, s32[128]{0:T(128)}, u32[]{:S(2)}) copy-start(s32[128]{0:T(128)} %param.13) | copy-start | bytes 1540
  0.0 0.7 %copy-start.6 = (s32[8]{0:T(128)S(1)}, s32[8]{0:T(128)}, u32[]{:S(2)}) copy-start(s32[8]{0:T(128)} %param.14) | copy-start | bytes 100
  0.7 0.9 %copy-start = (bf16[40,1024]{1,0:T(8,128)(2,1)S(1)}, bf16[40,1024]{1,0:T(8,128)(2,1)}, u32[]{:S(2)}) copy-start(bf16[40,1024]{1,0:T(8,128)(2,1)} %ker_ref.1) | copy-start | bytes 245764
  1.6 0.7 %copy-start.1 = (f32[40,128]{1,0:T(8,128)S(1)}, f32[40,128]{1,0:T(8,128)}, u32[]{:S(2)}) copy-start(f32[40,128]{1,0:T(8,128)} %wig_ref.1) | copy-start | bytes 61444
  2.3 0.7 %copy-start.2 = (bf16[8,1024]{1,0:T(8,128)(2,1)S(1)}, bf16[8,1024]{1,0:T(8,128)(2,1)}, u32[]{:S(2)}) copy-start(bf16[8,1024]{1,0:T(8,128)(2,1)} %rad_ref.1) | copy-start | bytes 49156
  3.0 0.7 %copy-start.3 = (bf16[32,128]{1,0:T(8,128)(2,1)S(1)}, bf16[32,128]{1,0:T(8,128)(2,1)}, u32[]{:S(2)}) copy-start(bf16[32,128]{1,0:T(8,128)(2,1)} %src_ref.1) | copy-start | bytes 24580

commit v2 on v1

--- a/solution.py
+++ b/solution.py
@@ -12,6 +12,7 @@
 F32 = jnp.float32
 I32 = jnp.int32
 LANES = 128
+ROOM = 60 << 20
 
 
 def grid_of(n):
@@ -26,8 +27,9 @@
 
 
 def kernel(
-    n, rad_ref, ker_ref, wig_ref, src_ref, slot_ref, own_ref, deg_ref, freq_ref,
-    out_ref, fbuf, pbuf, send_sem, recv_sem,
+    n, rad_hbm, ker_hbm, wig_hbm, src_hbm, slot_hbm, own_hbm, deg_hbm, freq_hbm, out_ref,
+    rad_ref, ker_ref, wig_ref, src_ref, slot_ref, own_ref, deg_ref, freq_ref,
+    fbuf, pbuf, load_sem, send_sem, recv_sem,
 ):
     outer, inner = grid_of(n)
     me = lax.axis_index("row")
@@ -45,63 +47,52 @@
     def at_in(step):
         return lax.rem(my_in + step, inner)
 
-    out_peers = [index(at_out(t), my_in, core) for t in range(1, outer)]
-    in_peers = [index(my_out, at_in(t), core) for t in range(1, inner)]
-    sibling = index(my_out, my_in, 1 - core)
+    outs = [at_out(t) for t in range(1, outer)]
+    ins = [at_in(t) for t in range(1, inner)]
+    other = 1 - core
+    every = slice(None)
+    sibling = index(my_out, my_in, other)
+    out_peers = [index(o, my_in, core) for o in outs]
+    in_peers = [index(my_out, i, core) for i in ins]
     peers = out_peers + in_peers + [sibling]
 
     barrier = pltpu.get_barrier_semaphore()
     for peer in peers:
         pl.semaphore_signal(barrier, inc=1, device_id={"row": peer}, device_id_type=MESH)
 
+    sources = (rad_hbm, deg_hbm, wig_hbm, slot_hbm, own_hbm, src_hbm, ker_hbm, freq_hbm)
+    held = (rad_ref, deg_ref, wig_ref, slot_ref, own_ref, src_ref, ker_ref, freq_ref)
+    loads = [
+        pltpu.make_async_copy(here, there, load_sem.at[k])
+        for k, (here, there) in enumerate(zip(sources, held))
+    ]
+    for load in loads:
+        load.start()
+
     bufs = (fbuf, pbuf)
     started = []
     counts = [0, 0]
 
-    def send(part, slot, peer):
-        copy = pltpu.make_async_remote_copy(
-            src_ref=bufs[part].at[slot],
-            dst_ref=bufs[part].at[slot],
+    def describe(part, view, key, peer):
+        return pltpu.make_async_remote_copy(
+            src_ref=bufs[part].at[view],
+            dst_ref=bufs[part].at[view],
             send_sem=send_sem.at[part, counts[part]],
-            recv_sem=recv_sem.at[part, slot],
+            recv_sem=recv_sem.at[part, key],
             device_id={"row": peer},
             device_id_type=MESH,
         )
+
+    def send(part, view, key, peer):
+        copy = describe(part, view, key, peer)
         counts[part] += 1
         copy.start()
         started.append(copy)
 
-    def arrived(part, slot):
-        pltpu.make_async_remote_copy(
-            src_ref=bufs[part].at[slot],
-            dst_ref=bufs[part].at[slot],
-            send_sem=send_sem.at[part, 0],
-            recv_sem=recv_sem.at[part, slot],
-            device_id={"row": sibling},
-            device_id_type=MESH,
-        ).wait_recv()
-
-    def send_own(part):
-        for peer in out_peers + in_peers + [sibling]:
-            send(part, me, peer)
-
-    def pass_out(part):
-        for slot in out_peers:
-            arrived(part, slot)
-            for peer in in_peers + [sibling]:
-                send(part, slot, peer)
-
-    def pass_in(part):
-        for o in range(outer):
-            for i in range(1, inner):
-                slot = index(at_out(o), at_in(i), core)
-                arrived(part, slot)
-                send(part, slot, sibling)
-
-    def last(part):
-        for o in range(outer):
-            for i in range(inner):
-                arrived(part, index(at_out(o), at_in(i), 1 - core))
+    def arrived(part, view, key):
+        describe(part, view, key, sibling).wait_recv()
+
+    mine = (my_out, my_in, core)
 
     mult, nodes = rad_ref.shape
     num_degree, table = wig_ref.shape
@@ -110,18 +101,23 @@
     half_deg = num_degree // 2
     half_lanes = half_deg * nsrc
 
+    for load in loads[:2]:
+        load.wait()
     rad = rad_ref[...].astype(F32)
     deg_row = deg_ref[...].astype(F32)
     eye = lax.broadcasted_iota(I32, (mult, mult), 0) == lax.broadcasted_iota(I32, (mult, mult), 1)
     deg_col = jnp.sum(jnp.where(eye, deg_row, 0.0), axis=1, keepdims=True)
     deg_block = jnp.broadcast_to(deg_col, (mult, LANES))
-    fbuf[me, :, :half_nodes] = jnp.concatenate(
+    fbuf[my_out, my_in, core, :, :half_nodes] = jnp.concatenate(
         [rad[:, :half_nodes], rad[:, half_nodes:]], axis=0
     ).astype(BF16)
-    fbuf[me, :, half_nodes:] = jnp.concatenate([deg_block, deg_block], axis=0).astype(BF16)
+    fbuf[my_out, my_in, core, :, half_nodes:] = jnp.concatenate([deg_block, deg_block], axis=0).astype(BF16)
     pl.semaphore_wait(barrier, len(peers))
-    send_own(0)
-
+    for peer in in_peers:
+        send(0, mine, me, peer)
+
+    for load in loads[2:6]:
+        load.wait()
     hot = (lax.broadcasted_iota(I32, (table, width), 0) == slot_ref[...]).astype(F32).astype(BF16)
     wig_high, wig_low = halves(wig_ref[...])
     angular = jnp.dot(wig_high, hot, preferred_element_type=F32) + jnp.dot(
@@ -139,21 +135,37 @@
         dims,
         preferred_element_type=F32,
     )
-    pbuf[me] = jnp.concatenate(
+    pbuf[my_out, my_in, core] = jnp.concatenate(
         [own_part[:, :half_lanes], own_part[:, half_lanes:]], axis=0
     ).astype(BF16)
-    send_own(1)
-
-    pass_out(0)
-
+    for peer in out_peers:
+        send(1, mine, me, peer)
+
+    for load in loads[6:]:
+        load.wait()
     ker = ker_ref[...].astype(F32)
     weighted = (ker[:, None, :] * rad[None, :, :]).reshape(num_degree * mult, nodes).astype(BF16)
     placed = (angular[:, None, :] * member[None, :, :]).reshape(num_degree * mult, width)
     placed_high, placed_low = halves(placed)
 
-    pass_in(0)
-    pass_out(1)
-    last(0)
+    for i in ins:
+        arrived(0, (my_out, i, core), index(my_out, i, core))
+    for peer in out_peers:
+        send(0, (my_out, every, core), n + my_out, peer)
+    send(0, (my_out, every, core), n + outer + my_out, sibling)
+    for o in outs:
+        arrived(1, (o, my_in, core), index(o, my_in, core))
+    for peer in in_peers:
+        send(1, (every, my_in, core), n + my_in, peer)
+    send(1, (every, my_in, core), n + inner + my_in, sibling)
+    for o in outs:
+        arrived(0, (o, every, core), n + o)
+        send(0, (o, every, core), n + outer + o, sibling)
+    for i in ins:
+        arrived(1, (every, i, core), n + i)
+        send(1, (every, i, core), n + inner + i, sibling)
+    for o in [my_out] + outs:
+        arrived(0, (o, every, other), n + outer + o)
 
     far = n * 2 * mult
     funcs = fbuf[...].reshape(far, half_nodes + LANES)
@@ -186,8 +198,8 @@
         keep = (least[h][s % 2] <= s) & (total >= s)
         rows.append(jnp.where(keep, value, 0.0))
 
-    pass_in(1)
-    last(1)
+    for i in [my_in] + ins:
+        arrived(1, (every, i, other), n + inner + i)
 
     per = LANES // nsrc
     lane_of = lax.broadcasted_iota(I32, (per * mult, LANES), 1) // nsrc
@@ -198,7 +210,7 @@
         lhs = jnp.concatenate(
             [rows[h * half_deg + g * per + t] for h in range(2) for t in range(per)], axis=0
         ).astype(BF16)
-        rhs = pbuf[:, :, g * LANES:(g + 1) * LANES].reshape(far, LANES)
+        rhs = pbuf[..., g * LANES:(g + 1) * LANES].reshape(far, LANES)
         both = jnp.dot(lhs, rhs, preferred_element_type=F32)
         for h in range(2):
             pieces[h].append(jnp.where(diagonal, both[h * per * mult:(h + 1) * per * mult], 0.0))
@@ -222,24 +234,27 @@
     mult, nodes = radial_funcs.shape
     num_degree = kernels.shape[0]
     nsrc, width = sources.shape
+    outer, inner = grid_of(n)
+    arrays = (
+        radial_funcs, kernels, wigner, sources, wigner_slots.reshape(1, -1), owners.reshape(1, -1),
+        degrees.reshape(1, -1), frequencies.reshape(1, -1),
+    )
     return pl.pallas_call(
         functools.partial(kernel, n),
         out_shape=jax.ShapeDtypeStruct((nsrc, width), F32),
-        in_specs=[pl.BlockSpec(memory_space=pltpu.VMEM)] * 8,
+        in_specs=[pl.BlockSpec(memory_space=pltpu.HBM)] * len(arrays),
         out_specs=pl.BlockSpec(memory_space=pltpu.VMEM),
-        scratch_shapes=[
-            pltpu.VMEM((n, 2 * mult, nodes // 2 + LANES), BF16),
-            pltpu.VMEM((n, 2 * mult, num_degree * nsrc // 2), BF16),
-            pltpu.SemaphoreType.DMA((2, n - 1)),
-            pltpu.SemaphoreType.DMA((2, n)),
+        scratch_shapes=[pltpu.VMEM(a.shape, a.dtype) for a in arrays] + [
+            pltpu.VMEM((outer, inner, 2, 2 * mult, nodes // 2 + LANES), BF16),
+            pltpu.VMEM((outer, inner, 2, 2 * mult, num_degree * nsrc // 2), BF16),
+            pltpu.SemaphoreType.DMA((len(arrays),)),
+            pltpu.SemaphoreType.DMA((2, 2 * (outer + inner))),
+            pltpu.SemaphoreType.DMA((2, n + 2 * max(outer, inner))),
         ],
         compiler_params=pltpu.CompilerParams(
-            collective_id=0, has_side_effects=True, vmem_limit_bytes=(8 << 20) + n * (256 << 10)
+            collective_id=0, has_side_effects=True, vmem_limit_bytes=ROOM
         ),
-    )(
-        radial_funcs, kernels, wigner, sources, wigner_slots.reshape(1, -1), owners.reshape(1, -1),
-        degrees.reshape(1, -1), frequencies.reshape(1, -1),
-    )
+    )(*arrays)
 
 
 def solution(mesh):

time: 21.1 us -> 17.4 us (0.82)
  local copies, waits for them, and re-layouts: 4.32 us -> 1.32 us
  Pallas kernels: 16.4 us -> 15.7 us
    unnamed x17 -> x1, local copies, waits for them, and re-layouts: 4.32 us -> 1.32 us
    pallas_call x1, Pallas kernels: 16.4 us -> 15.7 us  [local(): pl.pallas_call(functools.partial(kernel, n), out_shape=jax.ShapeDtypeStru...]
where the time goes in v2:
time: 17.4 us; the launch traced here: 17.1 us
  Pallas kernels  15.7 us (90%)
  local copies, waits for them, and re-layouts  1.32 us (8%)
    pallas_call x1, Pallas kernels, local(): pl.pallas_call(functools.partial(kernel, n), out_shape=jax.ShapeDtypeStru...  15.7 us
    unnamed x1, local copies, waits for them, and re-layouts  1.32 us

profile of v2, /device:TPU:1, one launch (start us, length us, event | category | flops | bytes accessed | tf_op | source)
XLA Modules:
  0.0 17.1 jit_solution(9859734507236093996)
XLA Ops:
  0.0 15.7 %shard_map.82 = f32[32,128]{1,0:T(8,128)} custom-call(bf16[8,1024]{1,0:T(8,128)(2,1)} %rad_hbm.1, bf16[40,1024]{1,0:T(8,128)(2,1)} %ker_hbm.1, f32[40,128]{1,0:T(8,128)} %wig_hbm.1, bf16[32,128]{1,0:T(8,128)(2,1)} %src_hbm.1, s32[1,128]{1,0:T(1,128)} %bitcast.4, s32[1,128]{1,0:T(1,128)} %bitcast.5, s32[1,8]{1,0:T(1,128)} %bitcast.6, f32[1,128]{1,0:T(1,128)} %bitcast.7), custom_call_target="tpu_custom_call" | custom-call | tf_op jit(solution)/shard_map/pallas_call | solution.py:242
  15.7 1.3 %copy.10 = f32[32,128]{1,0:T(8,128)} copy(f32[32,128]{1,0:T(8,128)} %shard_map.82) | data formatting | bytes 32768

commit v3 on v2

--- a/solution.py
+++ b/solution.py
@@ -12,7 +12,6 @@
 F32 = jnp.float32
 I32 = jnp.int32
 LANES = 128
-ROOM = 60 << 20
 
 
 def grid_of(n):
@@ -112,9 +111,6 @@
         [rad[:, :half_nodes], rad[:, half_nodes:]], axis=0
     ).astype(BF16)
     fbuf[my_out, my_in, core, :, half_nodes:] = jnp.concatenate([deg_block, deg_block], axis=0).astype(BF16)
-    pl.semaphore_wait(barrier, len(peers))
-    for peer in in_peers:
-        send(0, mine, me, peer)
 
     for load in loads[2:6]:
         load.wait()
@@ -138,6 +134,9 @@
     pbuf[my_out, my_in, core] = jnp.concatenate(
         [own_part[:, :half_lanes], own_part[:, half_lanes:]], axis=0
     ).astype(BF16)
+    pl.semaphore_wait(barrier, len(peers))
+    for peer in in_peers:
+        send(0, mine, me, peer)
     for peer in out_peers:
         send(1, mine, me, peer)
 
@@ -252,9 +251,9 @@
             pltpu.SemaphoreType.DMA((2, n + 2 * max(outer, inner))),
         ],
         compiler_params=pltpu.CompilerParams(
-            collective_id=0, has_side_effects=True, vmem_limit_bytes=ROOM
+            collective_id=0, has_side_effects=True, vmem_limit_bytes=(8 << 20) + n * (256 << 10)
         ),
-    )(*arrays)
+    )(*[pltpu.with_memory_space_constraint(a, pltpu.HBM) for a in arrays])
 
 
 def solution(mesh):

time: 17.4 us -> 15.1 us (0.87)
  Pallas kernels: 15.7 us -> 14.3 us
  local copies, waits for them, and re-layouts: 1.32 us -> 0.61 us
    pallas_call x1, Pallas kernels: 15.7 us -> 14.3 us  [local(): pl.pallas_call(functools.partial(kernel, n), out_shape=jax.ShapeDtypeStru...]
    unnamed x1, local copies, waits for them, and re-layouts: 1.32 us -> 0.61 us
where the time goes in v3:
time: 15.1 us; the launch traced here: 14.9 us
  Pallas kernels  14.3 us (95%)
  local copies, waits for them, and re-layouts  0.61 us (4%)
    pallas_call x1, Pallas kernels, local(): pl.pallas_call(functools.partial(kernel, n), out_shape=jax.ShapeDtypeStru...  14.3 us
    unnamed x1, local copies, waits for them, and re-layouts  0.61 us

profile of v3, /device:TPU:1, one launch (start us, length us, event | category | flops | bytes accessed | tf_op | source)
XLA Modules:
  0.0 14.9 jit_solution(15146341372742096723)
XLA Ops:
  0.0 14.3 %shard_map.82 = f32[32,128]{1,0:T(8,128)S(1)} custom-call(bf16[8,1024]{1,0:T(8,128)(2,1)} %rad_hbm.1, bf16[40,1024]{1,0:T(8,128)(2,1)} %ker_hbm.1, f32[40,128]{1,0:T(8,128)} %wig_hbm.1, bf16[32,128]{1,0:T(8,128)(2,1)} %src_hbm.1, s32[1,128]{1,0:T(1,128)} %bitcast.4, s32[1,128]{1,0:T(1,128)} %bitcast.5, s32[1,8]{1,0:T(1,128)} %bitcast.6, f32[1,128]{1,0:T(1,128)} %bitcast.7), custom_call_target="tpu_custom_call" | custom-call | tf_op jit(solution)/shard_map/pallas_call | solution.py:241
  14.3 0.6 %copy.10 = f32[32,128]{1,0:T(8,128)} copy(f32[32,128]{1,0:T(8,128)S(1)} %shard_map.82) | data formatting | bytes 32768
